TPU v7x, 32 devices: a whole 2x2x4 slice. The times are simulated.
32 devices in a mesh: row: 8 (over y, x, core), col: 4 (over z).
Axes of the slice: x: 2, y: 2, z: 4, core: 2. Of those that a mesh axis runs over, the one named last changes fastest.
Arguments:
- tokens: bfloat16 [512, 8192], P('col', 'row'), may hold values from -6 to 6
- w_packed: bfloat16 [8, 4, 448, 128, 128], P('row', 'col'), may hold values from -0.09375 to 0.09375
- kept_rows: int32 [8, 4, 448], P('row', 'col'), may hold values from 0 to 7, as said below
- kept_cols: int32 [8, 4, 448], P('row', 'col'), may hold values from 0 to 55, as said below
- kept_count: int32 [8, 4], P('row', 'col'), may hold values from 1 to 448, as said below
- grad_act: bfloat16 [512, 28672], P('row', 'col'), may hold values from -6 to 6
Outputs:
- activation: bfloat16 [512, 28672], P('row', 'col')
- input_grad: bfloat16 [512, 8192], P('col', 'row')
- weight_grad: bfloat16 [8, 4, 448, 128, 128], P('row', 'col')
Inputs may be any that keep to these rules, and one draw needn't show every extreme that they name: Within each tile, the 448 slots name every block of the tile once (kept_rows[r, c, s] * 56 + kept_cols[r, c, s] runs over all block places). `kept_cols`: see kept_rows. `kept_count`: some tile in every draw keeps all 448 blocks.
All inputs are finite; a program needn't handle non-finite values.
Results may differ from a plain program's by a relative error of at most 0.0049.
Values may be sent and summed in bfloat16 or wider, within the bound.
No kernel may reach another device: no remote copies, remote signals or barrier semaphores. Data moves between devices by JAX's collectives and lax.ppermute only.
A program may use at most 384 MiB of HBM per device.

v0:
```python
import jax
import jax.numpy as jnp
from jax import lax
from jax.sharding import PartitionSpec as P

gelu_scale = 0.7978845608
gelu_cubic = 0.044715


def gelu_pair(hidden, cotangent):
    inner = gelu_scale * (hidden + gelu_cubic * hidden * hidden * hidden)
    tangent = jnp.tanh(inner)
    activation = (0.5 * hidden * (1.0 + tangent)).astype(jnp.bfloat16)
    slope = 0.5 * (1.0 + tangent) + 0.5 * hidden * (1.0 - tangent * tangent) * gelu_scale * (
        1.0 + 3.0 * gelu_cubic * hidden * hidden
    )
    slope_grad = (cotangent.astype(jnp.float32) * slope).astype(jnp.bfloat16)
    return (activation, slope_grad)


def on_device(tokens, w_packed, kept_rows, kept_cols, kept_count, grad_act):
    block_size = w_packed.shape[-1]
    slot_count = w_packed.shape[2]
    width_here = tokens.shape[1]
    hidden_here = grad_act.shape[1]
    row_blocks = width_here // block_size
    col_blocks = hidden_here // block_size
    live_slots = jnp.arange(slot_count) < kept_count[0, 0]
    row_pick = (
        (kept_rows[0, 0][:, None] == jnp.arange(row_blocks)[None, :]) & live_slots[:, None]
    ).astype(jnp.bfloat16)
    col_pick = (
        (kept_cols[0, 0][:, None] == jnp.arange(col_blocks)[None, :]) & live_slots[:, None]
    ).astype(jnp.bfloat16)
    weight_blocks = w_packed[0, 0]
    gathered = lax.all_gather(tokens, "col", axis=0, tiled=True)

    def pick_rows(features, rows_here):
        shaped = features.reshape(rows_here, row_blocks, block_size)
        return jnp.einsum(
            "nrk,sr->nsk", shaped, row_pick, preferred_element_type=jnp.float32
        ).astype(jnp.bfloat16)

    def pick_cols(hidden_rows, rows_here):
        shaped = hidden_rows.reshape(rows_here, col_blocks, block_size)
        return jnp.einsum(
            "ncj,sc->nsj", shaped, col_pick, preferred_element_type=jnp.float32
        ).astype(jnp.bfloat16)

    rows_here = grad_act.shape[0] * lax.axis_size("row")
    features = gathered
    product = jnp.einsum(
        "nsk,skj->nsj",
        pick_rows(features, rows_here),
        weight_blocks,
        preferred_element_type=jnp.float32,
    )
    placed = jnp.einsum(
        "nsj,sc->ncj", product, col_pick.astype(jnp.float32), precision=lax.Precision.HIGHEST
    )
    hidden = lax.psum_scatter(
        placed.reshape(rows_here, hidden_here), "row", scatter_dimension=0, tiled=True
    )
    activation, slope_grad = gelu_pair(hidden, grad_act)
    grad_all = lax.all_gather(slope_grad, "row", axis=0, tiled=True)
    rows_here = grad_all.shape[0]
    weight_sum = jnp.einsum(
        "nsi,nsj->sij",
        pick_rows(gathered, rows_here),
        pick_cols(grad_all, rows_here),
        preferred_element_type=jnp.float32,
    )
    rows_here = grad_all.shape[0]
    product = jnp.einsum(
        "nsj,sij->nsi",
        pick_cols(grad_all, rows_here),
        weight_blocks,
        preferred_element_type=jnp.float32,
    )
    placed = jnp.einsum(
        "nsi,sr->nri", product, row_pick.astype(jnp.float32), precision=lax.Precision.HIGHEST
    )
    input_grad = lax.psum_scatter(
        placed.reshape(rows_here, width_here), "col", scatter_dimension=0, tiled=True
    ).astype(jnp.bfloat16)
    weight_grad = weight_sum.astype(jnp.bfloat16)[None, None]
    return (activation, input_grad, weight_grad)


def solution(mesh):
    placed = (
        P("col", "row"),
        P("row", "col", None, None, None),
        P("row", "col", None),
        P("row", "col", None),
        P("row", "col"),
        P("row", "col"),
    )
    return jax.shard_map(
        on_device,
        mesh=mesh,
        in_specs=placed,
        out_specs=(P("row", "col"), P("col", "row"), P("row", "col", None, None, None)),
        check_vma=False,
    )
```

profile of v0, /device:TPU:0, one launch (start us, length us, event | category | flops | bytes accessed | tf_op | source)
XLA Modules:
  0.0 833.2 jit_solution(6014442125814465879)
XLA Ops:
  7.2 0.0 all-gather.3.cloned.1.call-start
  7.2 0.7 all-gather.3.cloned.1.call-update
  7.9 0.0 reduce-scatter.3.cloned.1.call-start
  8.6 31.6 %all-gather.3.cloned.1.call-done = bf16[512,1024]{1,0:T(8,128)(2,1)} async-done(((bf16[128,1024]{1,0:T(8,128)(2,1)}), bf16[512,1024]{1,0:T(8,128)(2,1)}) %all-gather.3.cloned.1.call-update) | async-done | bytes 1048592 | tf_op jit(solution)/shard_map/all_gather | solution.py:36
  40.2 1.5 copy.14
  41.7 23.4 %convert_bitcast_fusion.1 = bf16[512,448,128]{2,1,0:T(8,128)(2,1)} fusion(bf16[512,8,128]{2,1,0:T(8,128)(2,1)S(1)} %bitcast.67, s32[448]{0:T(512)} %bitcast.71, pred[448]{0:T(512)(128)(4,1)S(1)} %iota_compare_fusion.2), kind=kOutput, calls=%fused_computation.7 | convolution fusion | flops 499129344 | bytes 59771072 | tf_op jit(solution)/shard_map/nrk,sr->nsk/dot_general | solution.py:40
  65.1 74.3 %copy.9 = bf16[512,448,128]{0,2,1:T(8,128)(2,1)} copy(bf16[512,448,128]{2,1,0:T(8,128)(2,1)} %convert_bitcast_fusion.1) | data formatting | bytes 117440512 | tf_op jit(solution)/shard_map/convert_element_type | solution.py:42
  139.4 0.0 copy-start.1
  139.4 63.2 %fusion.11 = f32[448,512,128]{2,1,0:T(8,128)} fusion(bf16[512,448,128]{0,2,1:T(8,128)(2,1)} %copy.9, bf16[1,1,448,128,128]{4,3,2,1,0:T(8,128)(2,1)} %param.7), kind=kOutput, calls=%fused_computation.14 | convolution fusion | flops 7516192768 | bytes 190840832 | tf_op jit(solution)/shard_map/nsk,skj->nsj/dot_general | solution.py:52
  202.7 0.0 copy-done.1
  202.7 150.7 %fusion.2 = f32[56,512,128]{2,0,1:T(8,128)} fusion(f32[448,512,128]{2,1,0:T(8,128)} %fusion.11, s32[448]{0:T(512)S(1)} %bitcast.69, pred[448]{0:T(512)(128)(4,1)S(1)} %iota_compare_fusion.2), kind=kOutput, calls=%fused_computation.2 | convolution fusion | flops 19730055168 | bytes 132122816 | tf_op jit(solution)/shard_map/nsj,sc->ncj/dot_general | solution.py:58
  353.4 13.6 %copy.36 = f32[64,8,56,128]{3,1,2,0:T(8,128)} copy(f32[64,8,56,128]{3,2,1,0:T(8,128)} %bitcast.61) | data formatting | bytes 29360128
  366.9 0.0 copy-start
  366.9 0.0 reduce-scatter.3.cloned.1.call-update
  367.0 0.0 all-gather.5.cloned.1.call-start
  367.0 103.1 %reduce-scatter.3.cloned.1.call-done = f32[64,7168]{1,0:T(8,128)} async-done(((f32[512,7168]{1,0:T(8,128)}), f32[64,7168]{1,0:T(8,128)}) %reduce-scatter.3.cloned.1.call-update) | async-done | bytes 1835024 | tf_op jit(solution)/shard_map/reduce_scatter | solution.py:61
  470.2 0.0 copy-done
  470.2 4.0 fusion.21
  474.2 0.0 all-gather.5.cloned.1.call-update
  474.2 0.0 reduce-scatter.5.cloned.1.call-start
  474.3 50.1 %all-gather.5.cloned.1.call-done = bf16[512,7168]{1,0:T(8,128)(2,1)} async-done(((bf16[64,7168]{1,0:T(8,128)(2,1)}), bf16[512,7168]{1,0:T(8,128)(2,1)}) %all-gather.5.cloned.1.call-update) | async-done | bytes 7340048 | tf_op jit(solution)/shard_map/all_gather | solution.py:65
  524.3 8.2 copy.16
  532.5 25.0 %convert_bitcast_fusion = bf16[512,448,128]{2,1,0:T(8,128)(2,1)} fusion(bf16[512,56,128]{2,1,0:T(8,128)(2,1)} %bitcast.63, s32[448]{0:T(512)S(1)} %bitcast.70, pred[448]{0:T(512)(128)(4,1)S(1)} %iota_compare_fusion.2), kind=kOutput, calls=%fused_computation.6 | convolution fusion | flops 3317744640 | bytes 66062528 | tf_op jit(solution)/shard_map/ncj,sc->nsj/dot_general | solution.py:46
  557.5 0.0 copy-start.2
  557.5 64.9 %fusion.6 = f32[448,512,128]{2,1,0:T(8,128)} fusion(bf16[512,448,128]{2,1,0:T(8,128)(2,1)} %convert_bitcast_fusion, bf16[1,1,448,128,128]{4,3,2,1,0:T(8,128)(2,1)} %param.7), kind=kOutput, calls=%fused_computation.8 | convolution fusion | flops 7516192768 | bytes 190840832 | tf_op jit(solution)/shard_map/nsj,sij->nsi/dot_general | solution.py:74
  622.4 0.0 copy-done.2
  622.4 68.8 %fusion = f32[8,512,128]{2,0,1:T(8,128)S(1)} fusion(f32[448,512,128]{2,1,0:T(8,128)} %fusion.6, s32[448]{0:T(512)S(1)} %bitcast.72, pred[448]{0:T(512)(128)(4,1)S(1)} %iota_compare_fusion.2), kind=kOutput, calls=%fused_computation | convolution fusion | flops 2818579456 | bytes 119539904 | tf_op jit(solution)/shard_map/nsi,sr->nri/dot_general | solution.py:80
  691.3 1.8 copy.37
  693.1 0.0 reduce-scatter.5.cloned.1.call-update
  693.1 131.4 %convert_bitcast_fusion.2 = bf16[1,1,448,128,128]{4,3,2,1,0:T(8,128)(2,1)} fusion(bf16[512,448,128]{0,2,1:T(8,128)(2,1)} %copy.9, bf16[512,448,128]{2,1,0:T(8,128)(2,1)} %convert_bitcast_fusion), kind=kOutput, calls=%fused_computation.16 | convolution fusion | flops 7523532800 | bytes 132120576 | tf_op jit(solution)/shard_map/nsi,nsj->sij/dot_general | solution.py:67
  824.5 0.0 reduce-scatter.5.cloned.1.call-done
  824.5 1.8 convert_element_type.40
  (1 shorter events, 0.0 us)
Async XLA Ops:
  7.2 33.1 %all-gather.3.cloned.1.call-start = ((), (), s32[]{:S(2)}) async-start(), calls=%async_computation.2 | async-start | bytes 1310720 | tf_op jit(solution)/shard_map/all_gather | solution.py:36
  7.9 462.3 %reduce-scatter.3.cloned.1.call-start = ((), (), s32[]{:S(2)}) async-start(), calls=%async_computation.3 | async-start | bytes 16515072 | tf_op jit(solution)/shard_map/reduce_scatter | solution.py:61
  139.4 63.2 %copy-start.1 = (s32[1,1,448]{2,1,0:T(1,128)S(1)}, s32[1,1,448]{2,1,0:T(1,128)}, u32[]{:S(2)}) copy-start(s32[1,1,448]{2,1,0:T(1,128)} %param.9) | copy-start | bytes 5380
  366.9 103.2 %copy-start = (bf16[64,7168]{1,0:T(8,128)(2,1)S(1)}, bf16[64,7168]{1,0:T(8,128)(2,1)}, u32[]{:S(2)}) copy-start(bf16[64,7168]{1,0:T(8,128)(2,1)} %param.11) | copy-start | bytes 2752516
  367.0 157.4 %all-gather.5.cloned.1.call-start = ((), (), s32[]{:S(2)}) async-start(), calls=%async_computation.4 | async-start | bytes 8257536 | tf_op jit(solution)/shard_map/all_gather | solution.py:65
  474.2 350.3 %reduce-scatter.5.cloned.1.call-start = ((), (), s32[]{:S(2)}) async-start(), calls=%async_computation.5 | async-start | bytes 2621440 | tf_op jit(solution)/shard_map/reduce_scatter | solution.py:83
  557.5 64.9 %copy-start.2 = (s32[1,1,448]{2,1,0:T(1,128)S(1)}, s32[1,1,448]{2,1,0:T(1,128)}, u32[]{:S(2)}) copy-start(s32[1,1,448]{2,1,0:T(1,128)} %param.8) | copy-start | bytes 5380
Sparse Core Ops, SparseCore 0:
  9.6 30.6 all-gather.2
  367.1 103.0 reduce-scatter.2
  474.3 49.9 all-gather.4
  693.2 43.8 reduce-scatter.4
where the time goes:
time: 841 us; the launch traced here: 833 us
  matrix products  527 us (63%)
  waiting for transfers between devices  186 us (22%)
  local copies, waits for them, and re-layouts  99.4 us (12%)
  between operations  14.8 us (2%)
    dot_general x1, matrix products, on_device(): jnp.einsum('nsj,sc->ncj', product, col_pick.astype(jnp.float32), precisio...  151 us
    dot_general x1, matrix products, on_device(): jnp.einsum('nsi,nsj->sij', pick_rows(gathered, rows_here), pick_cols(grad...  131 us
    reduce_scatter x1, waiting for transfers between devices, on_device(): lax.psum_scatter(placed.reshape(rows_here, hidden_here), 'row', scatter_d...  103 us
    convert_element_type x1, local copies, waits for them, and re-layouts, pick_rows(): return jnp.einsum('nrk,sr->nsk', shaped, row_pick, preferred_element_type...  74.3 us
    dot_general x1, matrix products, on_device(): jnp.einsum('nsi,sr->nri', product, row_pick.astype(jnp.float32), precisio...  68.8 us
    dot_general x1, matrix products, on_device(): jnp.einsum('nsj,sij->nsi', pick_cols(grad_all, rows_here), weight_blocks,...  64.9 us
    dot_general x1, matrix products, on_device(): jnp.einsum('nsk,skj->nsj', pick_rows(features, rows_here), weight_blocks,...  63.2 us
    all_gather x1, waiting for transfers between devices, on_device(): grad_all = lax.all_gather(slope_grad, 'row', axis=0, tiled=True)  50.1 us
  transfers between devices with their start and end apart: 4, of which 3 were waited for; matrix products, arithmetic and copies ran while one was open for 16% of the time, Pallas kernels for 0%

commit v1 on v0

v1 whole, which is shorter than its diff:
```python
import functools

import jax
import jax.numpy as jnp
import numpy as np
from jax import lax
from jax.experimental import pallas as pl
from jax.experimental.pallas import tpu as pltpu
from jax.sharding import PartitionSpec as P

gelu_scale = 0.7978845608
gelu_cubic = 0.044715
chunk_goal = 4
vmem_limit = 56 * 1024 * 1024


def gelu_pair(hidden, cotangent):
    inner = gelu_scale * (hidden + gelu_cubic * hidden * hidden * hidden)
    tangent = jnp.tanh(inner)
    activation = (0.5 * hidden * (1.0 + tangent)).astype(jnp.bfloat16)
    slope = 0.5 * (1.0 + tangent) + 0.5 * hidden * (1.0 - tangent * tangent) * gelu_scale * (
        1.0 + 3.0 * gelu_cubic * hidden * hidden
    )
    slope_grad = (cotangent.astype(jnp.float32) * slope).astype(jnp.bfloat16)
    return (activation, slope_grad)


def group_of(blocks, goal):
    return max(n for n in range(1, goal + 1) if blocks % n == 0)


def dense_kernel(row_blocks, col_blocks, per_step, depth, code, w_ref, out_ref, held, empty, sems):
    step = pl.program_id(0)
    steps = pl.num_programs(0)
    blk = w_ref.shape[-1]

    def load(at):
        slot_at = lax.rem(at, depth)
        for r in range(row_blocks):
            for c in range(per_step):
                entry = code[r * col_blocks + at * per_step + c]
                target = held.at[slot_at, pl.ds(r * blk, blk), pl.ds(c * blk, blk)]

                @pl.when(lax.rem(entry, 2) == 1)
                def _():
                    pltpu.make_async_copy(
                        w_ref.at[0, 0, lax.div(entry, 2)], target, sems.at[slot_at]
                    ).start()

                @pl.when(lax.rem(entry, 2) == 0)
                def _():
                    pltpu.make_async_copy(empty, target, sems.at[slot_at]).start()

    @pl.when(step == 0)
    def _():
        empty[...] = jnp.zeros_like(empty)
        for ahead in range(min(depth - 1, col_blocks // per_step)):
            load(jnp.int32(ahead))

    @pl.when(step + depth - 1 < steps)
    def _():
        load(step + depth - 1)

    slot_here = lax.rem(step, depth)
    pltpu.make_async_copy(held.at[slot_here], held.at[slot_here], sems.at[slot_here]).wait()
    out_ref[...] = held[slot_here]


def dense_tile(w_packed, code, row_blocks, col_blocks):
    blk = w_packed.shape[-1]
    per_step = group_of(col_blocks, 4)
    depth = 4
    wide = per_step * blk
    tall = row_blocks * blk
    return pl.pallas_call(
        functools.partial(dense_kernel, row_blocks, col_blocks, per_step, depth),
        out_shape=jax.ShapeDtypeStruct((tall, col_blocks * blk), w_packed.dtype),
        grid_spec=pltpu.PrefetchScalarGridSpec(
            num_scalar_prefetch=1,
            grid=(col_blocks // per_step,),
            in_specs=[pl.BlockSpec(memory_space=pl.ANY)],
            out_specs=pl.BlockSpec((tall, wide), lambda j, code: (0, j)),
            scratch_shapes=[
                pltpu.VMEM((depth, tall, wide), w_packed.dtype),
                pltpu.VMEM((blk, blk), w_packed.dtype),
                pltpu.SemaphoreType.DMA((depth,)),
            ],
        ),
        compiler_params=pltpu.CompilerParams(vmem_limit_bytes=vmem_limit),
        name="dense_tile",
    )(code, w_packed)


def forward_kernel(groups, rows, pick, x_ref, w_ref, keep_ref, send_ref, xs_ref):
    @pl.when(pl.program_id(0) == 0)
    def _():
        for t in range(groups):
            xs_ref[pl.ds(t * rows, rows), :] = x_ref[pick[t]]

    half = groups * rows // 2
    product = jnp.dot(xs_ref[...], w_ref[...], preferred_element_type=jnp.float32)
    keep_ref[...] = product[:half]
    send_ref[...] = product[half:].astype(jnp.bfloat16)


def forward(features, weight, pick):
    groups, rows, tall = features.shape
    hidden_here = weight.shape[1]
    wide = 128 * group_of(hidden_here // 128, 8)
    half = groups * rows // 2
    return pl.pallas_call(
        functools.partial(forward_kernel, groups, rows),
        out_shape=(
            jax.ShapeDtypeStruct((half, hidden_here), jnp.float32),
            jax.ShapeDtypeStruct((half, hidden_here), jnp.bfloat16),
            jax.ShapeDtypeStruct((groups * rows, tall), features.dtype),
        ),
        grid_spec=pltpu.PrefetchScalarGridSpec(
            num_scalar_prefetch=1,
            grid=(hidden_here // wide,),
            in_specs=[
                pl.BlockSpec((groups, rows, tall), lambda j, pick: (0, 0, 0)),
                pl.BlockSpec((tall, wide), lambda j, pick: (0, j)),
            ],
            out_specs=[
                pl.BlockSpec((half, wide), lambda j, pick: (0, j)),
                pl.BlockSpec((half, wide), lambda j, pick: (0, j)),
                pl.BlockSpec((groups * rows, tall), lambda j, pick: (0, 0)),
            ],
        ),
        compiler_params=pltpu.CompilerParams(vmem_limit_bytes=vmem_limit),
        name="forward",
    )(pick, features, weight)


def input_kernel(groups, rows, place, near_ref, far_ref, w_ref, out_ref, total):
    step = pl.program_id(0)

    @pl.when(step == 0)
    def _():
        total[...] = jnp.zeros_like(total)

    grad = jnp.concatenate([near_ref[...], far_ref[...]], axis=0)
    total[...] += lax.dot_general(
        grad, w_ref[...], (((1,), (1,)), ((), ())), preferred_element_type=jnp.float32
    )

    @pl.when(step == pl.num_programs(0) - 1)
    def _():
        for i in range(groups):
            start = pl.multiple_of(place[i] * rows, rows)
            out_ref[pl.ds(i * rows, rows), :] = total[pl.ds(start, rows), :]


def input_partial(near, far, weight, place):
    half, hidden_here = near.shape
    tall = weight.shape[0]
    groups = place.shape[0]
    rows = 2 * half // groups
    wide = 128 * group_of(hidden_here // 128, 8)
    return pl.pallas_call(
        functools.partial(input_kernel, groups, rows),
        out_shape=jax.ShapeDtypeStruct((2 * half, tall), jnp.float32),
        grid_spec=pltpu.PrefetchScalarGridSpec(
            num_scalar_prefetch=1,
            grid=(hidden_here // wide,),
            in_specs=[
                pl.BlockSpec((half, wide), lambda j, place: (0, j)),
                pl.BlockSpec((half, wide), lambda j, place: (0, j)),
                pl.BlockSpec((tall, wide), lambda j, place: (0, j)),
            ],
            out_specs=pl.BlockSpec((2 * half, tall), lambda j, place: (0, 0)),
            scratch_shapes=[pltpu.VMEM((2 * half, tall), jnp.float32)],
        ),
        compiler_params=pltpu.CompilerParams(vmem_limit_bytes=vmem_limit),
        name="input_partial",
    )(place, near, far, weight)


def weight_kernel(row_blocks, col_blocks, per_step, chunks, code, *refs):
    xs = refs[:chunks]
    grads = refs[chunks : 3 * chunks]
    out_ref, turned, made, sems = refs[3 * chunks :]
    step = pl.program_id(0)
    steps = pl.num_programs(0)
    blk = made.shape[-1]
    slot_here = lax.rem(step, 2)
    per_slot = row_blocks * per_step

    def finish(at):
        pltpu.make_async_copy(
            made.at[at], out_ref.at[0, 0, pl.ds(0, per_slot)], sems.at[at]
        ).wait()

    @pl.when(step == 0)
    def _():
        turned[...] = jnp.concatenate([x[...] for x in xs], axis=0).T

    @pl.when(step >= 2)
    def _():
        finish(slot_here)

    grad = jnp.concatenate([g[...] for g in grads], axis=0)
    product = jnp.dot(turned[...], grad, preferred_element_type=jnp.float32)
    for r in range(row_blocks):
        for c in range(per_step):
            entry = code[r * col_blocks + step * per_step + c]
            live = (lax.rem(entry, 2) == 1).astype(jnp.float32)
            block = product[r * blk : (r + 1) * blk, c * blk : (c + 1) * blk] * live
            made[slot_here, r * per_step + c] = block.astype(made.dtype)
            pltpu.make_async_copy(
                made.at[slot_here, r * per_step + c],
                out_ref.at[0, 0, lax.div(entry, 2)],
                sems.at[slot_here],
            ).start()

    @pl.when(step == steps - 1)
    def _():
        finish(slot_here)

        @pl.when(steps > 1)
        def _():
            finish(1 - slot_here)


def weight_gradient(features, grads, code, row_blocks, col_blocks, blk):
    chunks = len(features)
    tall = features[0].shape[1]
    tokens_all = sum(x.shape[0] for x in features)
    per_step = group_of(col_blocks, 4)
    wide = per_step * blk
    return pl.pallas_call(
        functools.partial(weight_kernel, row_blocks, col_blocks, per_step, chunks),
        out_shape=jax.ShapeDtypeStruct((1, 1, row_blocks * col_blocks, blk, blk), jnp.bfloat16),
        grid_spec=pltpu.PrefetchScalarGridSpec(
            num_scalar_prefetch=1,
            grid=(col_blocks // per_step,),
            in_specs=[pl.BlockSpec(x.shape, lambda j, code: (0, 0)) for x in features]
            + [pl.BlockSpec((g.shape[0], wide), lambda j, code: (0, j)) for g in grads],
            out_specs=pl.BlockSpec(memory_space=pl.ANY),
            scratch_shapes=[
                pltpu.VMEM((tall, tokens_all), jnp.bfloat16),
                pltpu.VMEM((2, row_blocks * per_step, blk, blk), jnp.bfloat16),
                pltpu.SemaphoreType.DMA((2,)),
            ],
        ),
        compiler_params=pltpu.CompilerParams(vmem_limit_bytes=vmem_limit),
        name="weight_gradient",
    )(code, *features, *grads)


def span_of(bits):
    span = [0]
    for bit in reversed(bits):
        span = span + [s ^ bit for s in span]
    return span


def swap(array, axis, size, bit):
    return lax.ppermute(array, axis, [(i, i ^ bit) for i in range(size)])


def on_device(tokens, w_packed, kept_rows, kept_cols, kept_count, grad_act):
    blk = w_packed.shape[-1]
    slot_count = w_packed.shape[2]
    tall = tokens.shape[1]
    hidden_here = grad_act.shape[1]
    row_blocks = tall // blk
    col_blocks = hidden_here // blk
    n_row = lax.axis_size("row")
    n_col = lax.axis_size("col")
    row_me = lax.axis_index("row")
    col_me = lax.axis_index("col")
    row_tokens = grad_act.shape[0]
    col_groups = tokens.shape[0] // row_tokens
    chunks = group_of(max(1, row_tokens // 16), chunk_goal)
    rows = row_tokens // chunks
    direct = n_col <= 8

    places = kept_rows[0, 0] * col_blocks + kept_cols[0, 0]
    slots = jnp.arange(slot_count, dtype=jnp.int32)
    coded = slots * 2 + (slots < kept_count[0, 0]).astype(jnp.int32)
    code = jnp.sum(jnp.where(places[None, :] == slots[:, None], coded[None, :], 0), axis=1)

    parts = tokens.reshape(col_groups, chunks, rows, tall)
    features = []
    for k in range(chunks):
        mine = parts[:, k]
        if direct:
            arrived = [mine] + [swap(mine, "col", n_col, m) for m in range(1, n_col)]
            features.append(jnp.concatenate(arrived, axis=0))
        else:
            features.append(lax.all_gather(mine, "col", axis=0, tiled=True))
    weight = dense_tile(w_packed, code, row_blocks, col_blocks)

    core_first = [1 << b for b in range(n_row.bit_length() - 1)]
    orders = [core_first, core_first[:1] + core_first[:0:-1]]
    picks, homes = [], []
    everyone = np.arange(n_row, dtype=np.int32)
    for bits in orders:
        owner = row_me ^ jnp.asarray(np.array(span_of(bits), np.int32))
        if direct:
            pick = (col_me ^ (owner // col_groups)) * col_groups + owner % col_groups
            home = (col_me ^ (everyone // col_groups)) * col_groups + everyone % col_groups
        else:
            pick = owner
            home = jnp.asarray(everyone)
        apart = row_me ^ home
        place = jnp.zeros_like(apart)
        for at, bit in enumerate(reversed(bits)):
            place = place + jnp.where((apart & bit) != 0, 1 << at, 0)
        picks.append(pick.astype(jnp.int32))
        homes.append(place.astype(jnp.int32))

    activations, near, far, sorted_features, input_grads = [], [], [], [], []
    for k in range(chunks):
        bits = orders[k % 2]
        keep, send, xs = forward(features[k], weight, picks[k % 2])
        sorted_features.append(xs)
        for at, bit in enumerate(bits):
            total = keep + swap(send, "row", n_row, bit).astype(jnp.float32)
            if at + 1 < len(bits):
                half = total.shape[0] // 2
                keep = total[:half]
                send = total[half:].astype(jnp.bfloat16)
        activation, slope_grad = gelu_pair(total, grad_act[k * rows : (k + 1) * rows])
        activations.append(activation)
        held = slope_grad
        for bit in reversed(bits):
            arrived = swap(held, "row", n_row, bit)
            if bit != bits[0]:
                held = jnp.concatenate([held, arrived], axis=0)
        near.append(held)
        far.append(arrived)
        partial = input_partial(held, arrived, weight, homes[k % 2])
        partial = partial.reshape(n_col, col_groups * rows, tall)
        if direct:
            total = partial[0]
            for m in range(1, n_col):
                total = total + swap(partial[m].astype(jnp.bfloat16), "col", n_col, m).astype(
                    jnp.float32
                )
        else:
            total = lax.psum_scatter(partial, "col", scatter_dimension=0, tiled=True)[0]
        input_grads.append(total.astype(jnp.bfloat16).reshape(col_groups, 1, rows, tall))
    weight_grad = weight_gradient(
        sorted_features,
        [g for pair in zip(near, far) for g in pair],
        code,
        row_blocks,
        col_blocks,
        blk,
    )
    activation = jnp.concatenate(activations, axis=0)
    input_grad = jnp.concatenate(input_grads, axis=1).reshape(tokens.shape)
    return (activation, input_grad, weight_grad)


def solution(mesh):
    placed = (
        P("col", "row"),
        P("row", "col", None, None, None),
        P("row", "col", None),
        P("row", "col", None),
        P("row", "col"),
        P("row", "col"),
    )
    return jax.shard_map(
        on_device,
        mesh=mesh,
        in_specs=placed,
        out_specs=(P("row", "col"), P("col", "row"), P("row", "col", None, None, None)),
        check_vma=False,
    )
```

time: 841 us -> 256 us (0.30)
  matrix products: 527 us -> 0 us
  waiting for transfers between devices: 186 us -> 52.7 us
  Pallas kernels: 0 us -> 118 us
  local copies, waits for them, and re-layouts: 99.4 us -> 3.65 us
  starting transfers between devices: 0.16 us -> 58 us
  other arithmetic: 5.81 us -> 19.3 us
  between operations: 14.8 us -> 1.74 us
    dot_general x7 -> x0, matrix products: 527 us -> none  [the longest x1 151 us: on_device(): jnp.einsum('nsj,sc->ncj', product, col_pick.astype(jnp.float32), precisio...]
    pallas_call x0 -> x10, Pallas kernels: none -> 118 us  [the longest x4 47.2 us: input_partial(): pl.pallas_call(functools.partial(input_kernel, groups, rows), out_shape=j...]
    reduce_scatter x2 -> x0, waiting for transfers between devices: 103 us -> none  [the longest x1 103 us: on_device(): lax.psum_scatter(placed.reshape(rows_here, hidden_here), 'row', scatter_d...]
    all_gather x2 -> x0, waiting for transfers between devices: 81.7 us -> none  [the longest x1 50.1 us: on_device(): grad_all = lax.all_gather(slope_grad, 'row', axis=0, tiled=True)]
    convert_element_type x1 -> x0, local copies, waits for them, and re-layouts: 74.3 us -> none  [pick_rows(): return jnp.einsum('nrk,sr->nsk', shaped, row_pick, preferred_element_type...]
    ppermute x0 -> x48, starting transfers between devices: none -> 58 us  [swap(): return lax.ppermute(array, axis, [(i, i ^ bit) for i in range(size)])]
    ppermute x0 -> x48, waiting for transfers between devices: none -> 52.7 us  [swap(): return lax.ppermute(array, axis, [(i, i ^ bit) for i in range(size)])]
    unnamed x10 -> x32, local copies, waits for them, and re-layouts: 25 us -> 1.61 us
  transfers between devices with their start and end apart: 4 -> 48, of which waited for: 3 -> 14; matrix products, arithmetic and copies ran while one was open for 16% -> 7% of each run, Pallas kernels for 0% -> 42%
where the time goes in v1:
time: 256 us; the launch traced here: 253 us
  Pallas kernels  118 us (46%)
  starting transfers between devices  58 us (23%)
  waiting for transfers between devices  52.7 us (21%)
  other arithmetic  19.3 us (8%)
  local copies, waits for them, and re-layouts  3.65 us (1%)
    ppermute x48, starting transfers between devices, swap(): return lax.ppermute(array, axis, [(i, i ^ bit) for i in range(size)])  58 us
    ppermute x48, waiting for transfers between devices, swap(): return lax.ppermute(array, axis, [(i, i ^ bit) for i in range(size)])  52.7 us
    pallas_call x4, Pallas kernels, input_partial(): pl.pallas_call(functools.partial(input_kernel, groups, rows), out_shape=j...  47.2 us
    pallas_call x4, Pallas kernels, forward(): pl.pallas_call(functools.partial(forward_kernel, groups, rows), out_shape...  42.8 us
    pallas_call x1, Pallas kernels, weight_gradient(): pl.pallas_call(functools.partial(weight_kernel, row_blocks, col_blocks, p...  16.2 us
    pallas_call x1, Pallas kernels, dense_tile(): pl.pallas_call(functools.partial(dense_kernel, row_blocks, col_blocks, pe...  11.5 us
  transfers between devices with their start and end apart: 48, of which 14 were waited for; matrix products, arithmetic and copies ran while one was open for 7% of the time, Pallas kernels for 42%

profile of v1, /device:TPU:0, one launch (start us, length us, event | category | flops | bytes accessed | tf_op | source)
XLA Modules:
  0.0 253.1 jit_solution(12912159132368025679)
XLA Ops:
  1.6 5.1 %collective-permute-start.20 = (bf16[2,16,1024]{2,1,0:T(8,128)(2,1)S(1)}, bf16[2,16,1024]{2,1,0:T(8,128)(2,1)S(1)}, u32[]{:S(2)}, u32[]{:S(2)}) collective-permute-start(bf16[2,16,1024]{2,1,0:T(8,128)(2,1)S(1)} %get-tuple-element.58), channel_id=1, source_target_pairs={{0,3},{1,2},{2,1},{3,0},{4,7},{5,6},{6,5},{7,4},{8,11},{9,10},{10,... | collective-permute-start | bytes 196616 | tf_op jit(solution)/shard_map/ppermute | solution.py:260
  10.7 11.5 %dense_tile.1.w_ref = bf16[1024,7168]{1,0:T(8,128)(2,1)} custom-call(s32[448]{0:T(512)} %select_reduce_fusion.code, bf16[1,1,448,128,128]{4,3,2,1,0:T(8,128)(2,1)} %w_ref.1), custom_call_target="tpu_custom_call" | custom-call | tf_op jit(solution)/shard_map/dense_tile/pallas_call | solution.py:75
  22.9 10.8 %forward.7 = (f32[64,7168]{1,0:T(8,128)}, bf16[64,7168]{1,0:T(8,128)(2,1)}, bf16[128,1024]{1,0:T(8,128)(2,1)}) custom-call(s32[8]{0:T(128)} %fusion.41.pick, bf16[8,16,1024]{2,1,0:T(8,128)(2,1)} %pad_maximum_fusion.12.x_ref, bf16[1024,7168]{1,0:T(8,128)(2,1)} %dense_tile.1.w_ref), custom_call_target="tpu_custom_call" | custom-call | tf_op jit(solution)/shard_map/forward/pallas_call | solution.py:111
  33.7 3.5 %collective-permute-start.8 = (bf16[2,16,1024]{2,1,0:T(8,128)(2,1)S(1)}, bf16[2,16,1024]{2,1,0:T(8,128)(2,1)S(1)}, u32[]{:S(2)}, u32[]{:S(2)}) collective-permute-start(bf16[2,16,1024]{2,1,0:T(8,128)(2,1)S(1)} %get-tuple-element.57), channel_id=1, source_target_pairs={{0,3},{1,2},{2,1},{3,0},{4,7},{5,6},{6,5},{7,4},{8,11},{9,10},{10,... | collective-permute-start | bytes 196616 | tf_op jit(solution)/shard_map/ppermute | solution.py:260
  38.1 3.5 %collective-permute-start.14 = (bf16[2,16,1024]{2,1,0:T(8,128)(2,1)S(1)}, bf16[2,16,1024]{2,1,0:T(8,128)(2,1)S(1)}, u32[]{:S(2)}, u32[]{:S(2)}) collective-permute-start(bf16[2,16,1024]{2,1,0:T(8,128)(2,1)S(1)} %get-tuple-element.56), channel_id=1, source_target_pairs={{0,3},{1,2},{2,1},{3,0},{4,7},{5,6},{6,5},{7,4},{8,11},{9,10},{10,... | collective-permute-start | bytes 196616 | tf_op jit(solution)/shard_map/ppermute | solution.py:260
  44.6 1.9 collective-permute-start.2
  47.3 10.6 %forward.5 = (f32[64,7168]{1,0:T(8,128)}, bf16[64,7168]{1,0:T(8,128)(2,1)}, bf16[128,1024]{1,0:T(8,128)(2,1)}) custom-call(s32[8]{0:T(128)} %fusion.41.pick, bf16[8,16,1024]{2,1,0:T(8,128)(2,1)} %pad_maximum_fusion.10.x_ref, bf16[1024,7168]{1,0:T(8,128)(2,1)} %dense_tile.1.w_ref), custom_call_target="tpu_custom_call" | custom-call | tf_op jit(solution)/shard_map/forward/pallas_call | solution.py:111
  61.1 10.7 %forward.6 = (f32[64,7168]{1,0:T(8,128)}, bf16[64,7168]{1,0:T(8,128)(2,1)}, bf16[128,1024]{1,0:T(8,128)(2,1)}) custom-call(s32[8]{0:T(128)} %fusion.40.pick, bf16[8,16,1024]{2,1,0:T(8,128)(2,1)} %pad_maximum_fusion.11.x_ref, bf16[1024,7168]{1,0:T(8,128)(2,1)} %dense_tile.1.w_ref), custom_call_target="tpu_custom_call" | custom-call | tf_op jit(solution)/shard_map/forward/pallas_call | solution.py:111
  73.1 10.7 %forward.4 = (f32[64,7168]{1,0:T(8,128)}, bf16[64,7168]{1,0:T(8,128)(2,1)}, bf16[128,1024]{1,0:T(8,128)(2,1)}) custom-call(s32[8]{0:T(128)} %fusion.40.pick, bf16[8,16,1024]{2,1,0:T(8,128)(2,1)} %pad_maximum_fusion.9.x_ref, bf16[1024,7168]{1,0:T(8,128)(2,1)} %dense_tile.1.w_ref), custom_call_target="tpu_custom_call" | custom-call | tf_op jit(solution)/shard_map/forward/pallas_call | solution.py:111
  87.7 2.2 collective-permute-start.16
  91.4 6.1 %collective-permute-done.22 = bf16[32,7168]{1,0:T(8,128)(2,1)S(1)} collective-permute-done((bf16[32,7168]{1,0:T(8,128)(2,1)S(1)}, bf16[32,7168]{1,0:T(8,128)(2,1)S(1)}, u32[]{:S(2)}, u32[]{:S(2)}) %collective-permute-start.22) | collective-permute-done | bytes 458784 | tf_op jit(solution)/shard_map/ppermute | solution.py:260
  97.6 2.5 collective-permute-start.23
  100.1 6.8 %collective-permute-done.10 = bf16[32,7168]{1,0:T(8,128)(2,1)S(1)} collective-permute-done((bf16[32,7168]{1,0:T(8,128)(2,1)S(1)}, bf16[32,7168]{1,0:T(8,128)(2,1)S(1)}, u32[]{:S(2)}, u32[]{:S(2)}) %collective-permute-start.10) | collective-permute-done | bytes 458784 | tf_op jit(solution)/shard_map/ppermute | solution.py:260
  107.0 2.5 collective-permute-start.11
  112.5 3.5 %collective-permute-done.23 = bf16[16,7168]{1,0:T(8,128)(2,1)S(1)} collective-permute-done((bf16[16,7168]{1,0:T(8,128)(2,1)S(1)}, bf16[16,7168]{1,0:T(8,128)(2,1)S(1)}, u32[]{:S(2)}, u32[]{:S(2)}) %collective-permute-start.23) | collective-permute-done | bytes 229408 | tf_op jit(solution)/shard_map/ppermute | solution.py:260
  115.9 4.6 %collective-permute-done.11 = bf16[16,7168]{1,0:T(8,128)(2,1)S(1)} collective-permute-done((bf16[16,7168]{1,0:T(8,128)(2,1)S(1)}, bf16[16,7168]{1,0:T(8,128)(2,1)S(1)}, u32[]{:S(2)}, u32[]{:S(2)}) %collective-permute-start.11) | collective-permute-done | bytes 229408 | tf_op jit(solution)/shard_map/ppermute | solution.py:260
  128.2 2.2 collective-permute-done.24
  131.7 2.4 collective-permute-done.30
  136.9 2.1 collective-permute-done.42
  139.7 16.4 %collective-permute-done.37 = bf16[32,7168]{1,0:T(8,128)(2,1)S(1)} collective-permute-done((bf16[32,7168]{1,0:T(8,128)(2,1)S(1)}, bf16[32,7168]{1,0:T(8,128)(2,1)S(1)}, u32[]{:S(2)}, u32[]{:S(2)}) %collective-permute-start.37) | collective-permute-done | bytes 458784 | tf_op jit(solution)/shard_map/ppermute | solution.py:260
  159.8 11.8 %input_partial.6 = f32[128,1024]{1,0:T(8,128)} custom-call(s32[8]{0:T(128)} %get-tuple-element.27.place, bf16[64,7168]{1,0:T(8,128)(2,1)} %copy-done, bf16[64,7168]{1,0:T(8,128)(2,1)} %copy-done.4, bf16[1024,7168]{1,0:T(8,128)(2,1)} %dense_tile.1.w_ref), custom_call_target="tpu_custom_call" | custom-call | tf_op jit(solution)/shard_map/input_partial/pallas_call | solution.py:161
  173.7 1.9 collective-permute-start.41
  176.5 11.8 %input_partial.7 = f32[128,1024]{1,0:T(8,128)} custom-call(s32[8]{0:T(128)} %fusion.45.place, bf16[64,7168]{1,0:T(8,128)(2,1)} %copy-done.1, bf16[64,7168]{1,0:T(8,128)(2,1)} %copy-done.5, bf16[1024,7168]{1,0:T(8,128)(2,1)} %dense_tile.1.w_ref), custom_call_target="tpu_custom_call" | custom-call | tf_op jit(solution)/shard_map/input_partial/pallas_call | solution.py:161
  191.1 11.8 %input_partial.5 = f32[128,1024]{1,0:T(8,128)} custom-call(s32[8]{0:T(128)} %fusion.45.place, bf16[64,7168]{1,0:T(8,128)(2,1)} %copy-done.2, bf16[64,7168]{1,0:T(8,128)(2,1)} %copy-done.6, bf16[1024,7168]{1,0:T(8,128)(2,1)} %dense_tile.1.w_ref), custom_call_target="tpu_custom_call" | custom-call | tf_op jit(solution)/shard_map/input_partial/pallas_call | solution.py:161
  204.0 2.0 collective-permute-start.47
  206.0 11.8 %input_partial.4 = f32[128,1024]{1,0:T(8,128)} custom-call(s32[8]{0:T(128)} %get-tuple-element.27.place, bf16[64,7168]{1,0:T(8,128)(2,1)} %copy-done.3, bf16[64,7168]{1,0:T(8,128)(2,1)} %copy-done.7, bf16[1024,7168]{1,0:T(8,128)(2,1)} %dense_tile.1.w_ref), custom_call_target="tpu_custom_call" | custom-call | tf_op jit(solution)/shard_map/input_partial/pallas_call | solution.py:161
  218.9 16.2 %weight_gradient.1 = bf16[1,1,448,128,128]{4,3,2,1,0:T(8,128)(2,1)} custom-call(s32[448]{0:T(512)} %select_reduce_fusion.code, bf16[128,1024]{1,0:T(8,128)(2,1)} %get-tuple-element.23.refs_0_, bf16[128,1024]{1,0:T(8,128)(2,1)} %get-tuple-element.24.refs_1_, bf16[128,1024]{1,0:T(8,128)(2,1)} %get-tuple-element.25.refs_2_, ...), custom_call_target="tpu_custom_call" | custom-call | tf_op jit(solution)/shard_map/weight_gradient/pallas_call | solution.py:232
  235.6 2.1 collective-permute-start.33
  237.6 1.9 collective-permute-start.35
  240.6 2.5 collective-permute-start.27
  246.0 2.0 collective-permute-done.34
  249.2 2.1 collective-permute-done.28
  (158 shorter events, 53.9 us)
Async XLA Ops:
  1.6 20.6 %collective-permute-start.20 = (bf16[2,16,1024]{2,1,0:T(8,128)(2,1)S(1)}, bf16[2,16,1024]{2,1,0:T(8,128)(2,1)S(1)}, u32[]{:S(2)}, u32[]{:S(2)}) collective-permute-start(bf16[2,16,1024]{2,1,0:T(8,128)(2,1)S(1)} %get-tuple-element.58), channel_id=1, source_target_pairs={{0,3},{1,2},{2,1},{3,0},{4,7},{5,6},{6,5},{7,4},{8,11},{9,10},{10,... | collective-permute-start | bytes 196616 | tf_op jit(solution)/shard_map/ppermute | solution.py:260
  6.7 15.5 %collective-permute-start.19 = (bf16[2,16,1024]{2,1,0:T(8,128)(2,1)S(1)}, bf16[2,16,1024]{2,1,0:T(8,128)(2,1)S(1)}, u32[]{:S(2)}, u32[]{:S(2)}) collective-permute-start(bf16[2,16,1024]{2,1,0:T(8,128)(2,1)S(1)} %get-tuple-element.58), channel_id=1, source_target_pairs={{0,2},{1,3},{2,0},{3,1},{4,6},{5,7},{6,4},{7,5},{8,10},{9,11},{10,... | collective-permute-start | bytes 196616 | tf_op jit(solution)/shard_map/ppermute | solution.py:260
  6.7 15.5 %collective-permute-start.18 = (bf16[2,16,1024]{2,1,0:T(8,128)(2,1)S(1)}, bf16[2,16,1024]{2,1,0:T(8,128)(2,1)S(1)}, u32[]{:S(2)}, u32[]{:S(2)}) collective-permute-start(bf16[2,16,1024]{2,1,0:T(8,128)(2,1)S(1)} %get-tuple-element.58), channel_id=1, source_target_pairs={{0,1},{1,0},{2,3},{3,2},{4,5},{5,4},{6,7},{7,6},{8,9},{9,8},{10,11... | collective-permute-start | bytes 196616 | tf_op jit(solution)/shard_map/ppermute | solution.py:260
  33.7 50.2 %collective-permute-start.21 = (bf16[64,7168]{1,0:T(8,128)(2,1)}, bf16[64,7168]{1,0:T(8,128)(2,1)S(1)}, u32[]{:S(2)}, u32[]{:S(2)}) collective-permute-start(bf16[64,7168]{1,0:T(8,128)(2,1)} %get-tuple-element.22), channel_id=1, source_target_pairs={{0,4},{4,0},{8,12},{12,8},{16,20},{20,16},{24,28},{28,24},{1,5},{5... | collective-permute-start | bytes 2752520 | tf_op jit(solution)/shard_map/ppermute | solution.py:260
  38.1 19.8 %collective-permute-start.14 = (bf16[2,16,1024]{2,1,0:T(8,128)(2,1)S(1)}, bf16[2,16,1024]{2,1,0:T(8,128)(2,1)S(1)}, u32[]{:S(2)}, u32[]{:S(2)}) collective-permute-start(bf16[2,16,1024]{2,1,0:T(8,128)(2,1)S(1)} %get-tuple-element.56), channel_id=1, source_target_pairs={{0,3},{1,2},{2,1},{3,0},{4,7},{5,6},{6,5},{7,4},{8,11},{9,10},{10,... | collective-permute-start | bytes 196616 | tf_op jit(solution)/shard_map/ppermute | solution.py:260
  42.1 16.7 %collective-permute-start.13 = (bf16[2,16,1024]{2,1,0:T(8,128)(2,1)S(1)}, bf16[2,16,1024]{2,1,0:T(8,128)(2,1)S(1)}, u32[]{:S(2)}, u32[]{:S(2)}) collective-permute-start(bf16[2,16,1024]{2,1,0:T(8,128)(2,1)S(1)} %get-tuple-element.56), channel_id=1, source_target_pairs={{0,2},{1,3},{2,0},{3,1},{4,6},{5,7},{6,4},{7,5},{8,10},{9,11},{10,... | collective-permute-start | bytes 196616 | tf_op jit(solution)/shard_map/ppermute | solution.py:260
  43.9 16.5 %collective-permute-start.12 = (bf16[2,16,1024]{2,1,0:T(8,128)(2,1)S(1)}, bf16[2,16,1024]{2,1,0:T(8,128)(2,1)S(1)}, u32[]{:S(2)}, u32[]{:S(2)}) collective-permute-start(bf16[2,16,1024]{2,1,0:T(8,128)(2,1)S(1)} %get-tuple-element.56), channel_id=1, source_target_pairs={{0,1},{1,0},{2,3},{3,2},{4,5},{5,4},{6,7},{7,6},{8,9},{9,8},{10,11... | collective-permute-start | bytes 196616 | tf_op jit(solution)/shard_map/ppermute | solution.py:260
  44.6 27.2 %collective-permute-start.2 = (bf16[2,16,1024]{2,1,0:T(8,128)(2,1)S(1)}, bf16[2,16,1024]{2,1,0:T(8,128)(2,1)S(1)}, u32[]{:S(2)}, u32[]{:S(2)}) collective-permute-start(bf16[2,16,1024]{2,1,0:T(8,128)(2,1)S(1)} %get-tuple-element.55), channel_id=1, source_target_pairs={{0,3},{1,2},{2,1},{3,0},{4,7},{5,6},{6,5},{7,4},{8,11},{9,10},{10,... | collective-permute-start | bytes 196616 | tf_op jit(solution)/shard_map/ppermute | solution.py:260
  57.9 14.4 %collective-permute-start.1 = (bf16[2,16,1024]{2,1,0:T(8,128)(2,1)S(1)}, bf16[2,16,1024]{2,1,0:T(8,128)(2,1)S(1)}, u32[]{:S(2)}, u32[]{:S(2)}) collective-permute-start(bf16[2,16,1024]{2,1,0:T(8,128)(2,1)S(1)} %get-tuple-element.55), channel_id=1, source_target_pairs={{0,2},{1,3},{2,0},{3,1},{4,6},{5,7},{6,4},{7,5},{8,10},{9,11},{10,... | collective-permute-start | bytes 196616 | tf_op jit(solution)/shard_map/ppermute | solution.py:260
  58.8 13.6 %collective-permute-start = (bf16[2,16,1024]{2,1,0:T(8,128)(2,1)S(1)}, bf16[2,16,1024]{2,1,0:T(8,128)(2,1)S(1)}, u32[]{:S(2)}, u32[]{:S(2)}) collective-permute-start(bf16[2,16,1024]{2,1,0:T(8,128)(2,1)S(1)} %get-tuple-element.55), channel_id=1, source_target_pairs={{0,1},{1,0},{2,3},{3,2},{4,5},{5,4},{6,7},{7,6},{8,9},{9,8},{10,11... | collective-permute-start | bytes 196616 | tf_op jit(solution)/shard_map/ppermute | solution.py:260
  60.4 25.5 %collective-permute-start.9 = (bf16[64,7168]{1,0:T(8,128)(2,1)}, bf16[64,7168]{1,0:T(8,128)(2,1)S(1)}, u32[]{:S(2)}, u32[]{:S(2)}) collective-permute-start(bf16[64,7168]{1,0:T(8,128)(2,1)} %get-tuple-element.18), channel_id=1, source_target_pairs={{0,4},{4,0},{8,12},{12,8},{16,20},{20,16},{24,28},{28,24},{1,5},{5... | collective-permute-start | bytes 2752520 | tf_op jit(solution)/shard_map/ppermute | solution.py:260
  71.8 15.6 %collective-permute-start.15 = (bf16[64,7168]{1,0:T(8,128)(2,1)}, bf16[64,7168]{1,0:T(8,128)(2,1)S(1)}, u32[]{:S(2)}, u32[]{:S(2)}) collective-permute-start(bf16[64,7168]{1,0:T(8,128)(2,1)} %get-tuple-element.20), channel_id=1, source_target_pairs={{0,4},{4,0},{8,12},{12,8},{16,20},{20,16},{24,28},{28,24},{1,5},{5... | collective-permute-start | bytes 2752520 | tf_op jit(solution)/shard_map/ppermute | solution.py:260
  84.1 13.4 %collective-permute-start.22 = (bf16[32,7168]{1,0:T(8,128)(2,1)S(1)}, bf16[32,7168]{1,0:T(8,128)(2,1)S(1)}, u32[]{:S(2)}, u32[]{:S(2)}) collective-permute-start(bf16[32,7168]{1,0:T(8,128)(2,1)S(1)} %slice.300), channel_id=1, source_target_pairs={{0,16},{4,20},{8,24},{12,28},{16,0},{20,4},{24,8},{28,12},{1,17},{... | collective-permute-start | bytes 1376264 | tf_op jit(solution)/shard_map/ppermute | solution.py:260
  86.2 20.7 %collective-permute-start.10 = (bf16[32,7168]{1,0:T(8,128)(2,1)S(1)}, bf16[32,7168]{1,0:T(8,128)(2,1)S(1)}, u32[]{:S(2)}, u32[]{:S(2)}) collective-permute-start(bf16[32,7168]{1,0:T(8,128)(2,1)S(1)} %slice.302), channel_id=1, source_target_pairs={{0,16},{4,20},{8,24},{12,28},{16,0},{20,4},{24,8},{28,12},{1,17},{... | collective-permute-start | bytes 1376264 | tf_op jit(solution)/shard_map/ppermute | solution.py:260
  87.7 21.8 %collective-permute-start.16 = (bf16[32,7168]{1,0:T(8,128)(2,1)S(1)}, bf16[32,7168]{1,0:T(8,128)(2,1)S(1)}, u32[]{:S(2)}, u32[]{:S(2)}) collective-permute-start(bf16[32,7168]{1,0:T(8,128)(2,1)S(1)} %slice.301), channel_id=1, source_target_pairs={{0,8},{4,12},{8,0},{12,4},{16,24},{20,28},{24,16},{28,20},{1,9},{5... | collective-permute-start | bytes 1376264 | tf_op jit(solution)/shard_map/ppermute | solution.py:260
  90.1 21.0 %collective-permute-start.4 = (bf16[32,7168]{1,0:T(8,128)(2,1)S(1)}, bf16[32,7168]{1,0:T(8,128)(2,1)S(1)}, u32[]{:S(2)}, u32[]{:S(2)}) collective-permute-start(bf16[32,7168]{1,0:T(8,128)(2,1)S(1)} %slice.303), channel_id=1, source_target_pairs={{0,8},{4,12},{8,0},{12,4},{16,24},{20,28},{24,16},{28,20},{1,9},{5... | collective-permute-start | bytes 1376264 | tf_op jit(solution)/shard_map/ppermute | solution.py:260
  97.6 18.3 %collective-permute-start.23 = (bf16[16,7168]{1,0:T(8,128)(2,1)S(1)}, bf16[16,7168]{1,0:T(8,128)(2,1)S(1)}, u32[]{:S(2)}, u32[]{:S(2)}) collective-permute-start(bf16[16,7168]{1,0:T(8,128)(2,1)S(1)} %slice.304), channel_id=1, source_target_pairs={{0,8},{4,12},{8,0},{12,4},{16,24},{20,28},{24,16},{28,20},{1,9},{5... | collective-permute-start | bytes 688136 | tf_op jit(solution)/shard_map/ppermute | solution.py:260
  107.0 13.4 %collective-permute-start.11 = (bf16[16,7168]{1,0:T(8,128)(2,1)S(1)}, bf16[16,7168]{1,0:T(8,128)(2,1)S(1)}, u32[]{:S(2)}, u32[]{:S(2)}) collective-permute-start(bf16[16,7168]{1,0:T(8,128)(2,1)S(1)} %slice.306), channel_id=1, source_target_pairs={{0,8},{4,12},{8,0},{12,4},{16,24},{20,28},{24,16},{28,20},{1,9},{5... | collective-permute-start | bytes 688136 | tf_op jit(solution)/shard_map/ppermute | solution.py:260
  109.6 10.8 %collective-permute-start.17 = (bf16[16,7168]{1,0:T(8,128)(2,1)S(1)}, bf16[16,7168]{1,0:T(8,128)(2,1)S(1)}, u32[]{:S(2)}, u32[]{:S(2)}) collective-permute-start(bf16[16,7168]{1,0:T(8,128)(2,1)S(1)} %slice.305), channel_id=1, source_target_pairs={{0,16},{4,20},{8,24},{12,28},{16,0},{20,4},{24,8},{28,12},{1,17},{... | collective-permute-start | bytes 688136 | tf_op jit(solution)/shard_map/ppermute | solution.py:260
  126.2 12.8 %collective-permute-start.42 = (bf16[16,7168]{1,0:T(8,128)(2,1)S(1)}, bf16[16,7168]{1,0:T(8,128)(2,1)S(1)}, u32[]{:S(2)}, u32[]{:S(2)}) collective-permute-start(bf16[16,7168]{1,0:T(8,128)(2,1)S(1)} %get-tuple-element.40), channel_id=1, source_target_pairs={{0,8},{4,12},{8,0},{12,4},{16,24},{20,28},{24,16},{28,20},{1,9},{5... | collective-permute-start | bytes 688136 | tf_op jit(solution)/shard_map/ppermute | solution.py:260
  130.5 26.7 %collective-permute-start.25 = (bf16[32,7168]{1,0:T(8,128)(2,1)S(1)}, bf16[32,7168]{1,0:T(8,128)(2,1)S(1)}, u32[]{:S(2)}, u32[]{:S(2)}) collective-permute-start(bf16[32,7168]{1,0:T(8,128)(2,1)S(1)} %pad_maximum_fusion.5), channel_id=1, source_target_pairs={{0,8},{4,12},{8,0},{12,4},{16,24},{20,28},{24,16},{28,20},{1,9},{5... | collective-permute-start | bytes 1376264 | tf_op jit(solution)/shard_map/ppermute | solution.py:260
  134.1 22.9 %collective-permute-start.31 = (bf16[32,7168]{1,0:T(8,128)(2,1)S(1)}, bf16[32,7168]{1,0:T(8,128)(2,1)S(1)}, u32[]{:S(2)}, u32[]{:S(2)}) collective-permute-start(bf16[32,7168]{1,0:T(8,128)(2,1)S(1)} %pad_maximum_fusion.6), channel_id=1, source_target_pairs={{0,16},{4,20},{8,24},{12,28},{16,0},{20,4},{24,8},{28,12},{1,17},{... | collective-permute-start | bytes 1376264 | tf_op jit(solution)/shard_map/ppermute | solution.py:260
  136.1 20.0 %collective-permute-start.37 = (bf16[32,7168]{1,0:T(8,128)(2,1)S(1)}, bf16[32,7168]{1,0:T(8,128)(2,1)S(1)}, u32[]{:S(2)}, u32[]{:S(2)}) collective-permute-start(bf16[32,7168]{1,0:T(8,128)(2,1)S(1)} %pad_maximum_fusion.7), channel_id=1, source_target_pairs={{0,8},{4,12},{8,0},{12,4},{16,24},{20,28},{24,16},{28,20},{1,9},{5... | collective-permute-start | bytes 1376264 | tf_op jit(solution)/shard_map/ppermute | solution.py:260
  139.0 17.3 %collective-permute-start.43 = (bf16[32,7168]{1,0:T(8,128)(2,1)S(1)}, bf16[32,7168]{1,0:T(8,128)(2,1)S(1)}, u32[]{:S(2)}, u32[]{:S(2)}) collective-permute-start(bf16[32,7168]{1,0:T(8,128)(2,1)S(1)} %pad_maximum_fusion.8), channel_id=1, source_target_pairs={{0,16},{4,20},{8,24},{12,28},{16,0},{20,4},{24,8},{28,12},{1,17},{... | collective-permute-start | bytes 1376264 | tf_op jit(solution)/shard_map/ppermute | solution.py:260
  156.4 19.2 %collective-permute-start.44 = (bf16[64,7168]{1,0:T(8,128)(2,1)S(1)}, bf16[64,7168]{1,0:T(8,128)(2,1)S(1)}, u32[]{:S(2)}, u32[]{:S(2)}) collective-permute-start(bf16[64,7168]{1,0:T(8,128)(2,1)S(1)} %pad_maximum_fusion.4.near_ref.refs_10_), channel_id=1, source_target_pairs={{0,4},{4,0},{8,12},{12,8},{16,20},{20,16},{24,28},{28,24},{1,5},{5... | collective-permute-start | bytes 2752520 | tf_op jit(solution)/shard_map/ppermute | solution.py:260
  157.2 32.3 %collective-permute-start.32 = (bf16[64,7168]{1,0:T(8,128)(2,1)S(1)}, bf16[64,7168]{1,0:T(8,128)(2,1)S(1)}, u32[]{:S(2)}, u32[]{:S(2)}) collective-permute-start(bf16[64,7168]{1,0:T(8,128)(2,1)S(1)} %pad_maximum_fusion.2.near_ref.refs_6_), channel_id=1, source_target_pairs={{0,4},{4,0},{8,12},{12,8},{16,20},{20,16},{24,28},{28,24},{1,5},{5... | collective-permute-start | bytes 2752520 | tf_op jit(solution)/shard_map/ppermute | solution.py:260
  157.5 46.5 %collective-permute-start.26 = (bf16[64,7168]{1,0:T(8,128)(2,1)S(1)}, bf16[64,7168]{1,0:T(8,128)(2,1)S(1)}, u32[]{:S(2)}, u32[]{:S(2)}) collective-permute-start(bf16[64,7168]{1,0:T(8,128)(2,1)S(1)} %pad_maximum_fusion.1.near_ref.refs_4_), channel_id=1, source_target_pairs={{0,4},{4,0},{8,12},{12,8},{16,20},{20,16},{24,28},{28,24},{1,5},{5... | collective-permute-start | bytes 2752520 | tf_op jit(solution)/shard_map/ppermute | solution.py:260
  172.8 62.3 %collective-permute-start.39 = (bf16[32,1024]{1,0:T(8,128)(2,1)S(1)}, bf16[32,1024]{1,0:T(8,128)(2,1)S(1)}, u32[]{:S(2)}, u32[]{:S(2)}) collective-permute-start(bf16[32,1024]{1,0:T(8,128)(2,1)S(1)} %get-tuple-element.49), channel_id=1, source_target_pairs={{0,1},{1,0},{2,3},{3,2},{4,5},{5,4},{6,7},{7,6},{8,9},{9,8},{10,11... | collective-permute-start | bytes 196616 | tf_op jit(solution)/shard_map/ppermute | solution.py:260
  173.7 61.9 %collective-permute-start.41 = (bf16[32,1024]{1,0:T(8,128)(2,1)S(1)}, bf16[32,1024]{1,0:T(8,128)(2,1)S(1)}, u32[]{:S(2)}, u32[]{:S(2)}) collective-permute-start(bf16[32,1024]{1,0:T(8,128)(2,1)S(1)} %get-tuple-element.50), channel_id=1, source_target_pairs={{0,3},{1,2},{2,1},{3,0},{4,7},{5,6},{6,5},{7,4},{8,11},{9,10},{10,... | collective-permute-start | bytes 196616 | tf_op jit(solution)/shard_map/ppermute | solution.py:260
  175.6 62.0 %collective-permute-start.40 = (bf16[32,1024]{1,0:T(8,128)(2,1)S(1)}, bf16[32,1024]{1,0:T(8,128)(2,1)S(1)}, u32[]{:S(2)}, u32[]{:S(2)}) collective-permute-start(bf16[32,1024]{1,0:T(8,128)(2,1)S(1)} %get-tuple-element.51), channel_id=1, source_target_pairs={{0,2},{1,3},{2,0},{3,1},{4,6},{5,7},{6,4},{7,5},{8,10},{9,11},{10,... | collective-permute-start | bytes 196616 | tf_op jit(solution)/shard_map/ppermute | solution.py:260
  189.5 51.0 %collective-permute-start.45 = (bf16[32,1024]{1,0:T(8,128)(2,1)S(1)}, bf16[32,1024]{1,0:T(8,128)(2,1)S(1)}, u32[]{:S(2)}, u32[]{:S(2)}) collective-permute-start(bf16[32,1024]{1,0:T(8,128)(2,1)S(1)} %get-tuple-element.52), channel_id=1, source_target_pairs={{0,1},{1,0},{2,3},{3,2},{4,5},{5,4},{6,7},{7,6},{8,9},{9,8},{10,11... | collective-permute-start | bytes 196616 | tf_op jit(solution)/shard_map/ppermute | solution.py:260
  204.0 36.5 %collective-permute-start.47 = (bf16[32,1024]{1,0:T(8,128)(2,1)S(1)}, bf16[32,1024]{1,0:T(8,128)(2,1)S(1)}, u32[]{:S(2)}, u32[]{:S(2)}) collective-permute-start(bf16[32,1024]{1,0:T(8,128)(2,1)S(1)} %get-tuple-element.53), channel_id=1, source_target_pairs={{0,3},{1,2},{2,1},{3,0},{4,7},{5,6},{6,5},{7,4},{8,11},{9,10},{10,... | collective-permute-start | bytes 196616 | tf_op jit(solution)/shard_map/ppermute | solution.py:260
  (32 other events, 217.3 us)
